TPU v7x, 512 devices: a whole 4x8x8 slice. The times are simulated.
512 devices in a mesh: region: 16 (over y, core), tile: 32 (over x, z).
Axes of the slice: x: 4, y: 8, z: 8, core: 2. Of those that a mesh axis runs over, the one named last changes fastest.
Arguments:
- prior_pressure: float32 [64, 4, 64, 4096], P(None, None, 'region', 'tile'), may hold values from -6 to 6
- infiltration_source: float32 [64, 64, 4096], P(None, 'region', 'tile'), may hold values from -6 to 6
- soil_class: int32 [4, 64, 4096], P(None, 'region', 'tile'), may hold values from 0 to 11
- soil_k: float32 [12], replicated, may hold values from 0.02 to 0.2
- obs_index: int32 [131072], P(('region', 'tile')), may hold values from 0 to 2047
- obs_value: float32 [131072], P(('region', 'tile')), may hold values from -6 to 6
- obs_var: float32 [131072], P(('region', 'tile')), may hold values from 0.5 to 8
- obs_count: int32 [512], P(('region', 'tile')), may hold values from 1 to 256, as said below
Outputs:
- analysis: float32 [64, 4, 64, 4096], P(None, None, 'region', 'tile')
Inputs may be any that keep to these rules, and one draw needn't show every extreme that they name: `obs_count`: at least one block has all 256 slots live.
All inputs are finite; a program needn't handle non-finite values.
Results may differ from a plain program's by a relative error of at most 0.00019.
Values sent between devices are 32-bit elements; how exact they have to be, the bound alone decides.
No kernel may reach another device: no remote copies, remote signals or barrier semaphores. Data moves between devices by JAX's collectives and lax.ppermute only.
A program may use at most 64 MiB of HBM per device.

v0:
```python
import jax
import jax.numpy as jnp
from jax import lax
from jax.sharding import PartitionSpec as P

STEPS = 3
step_dt = 0.25
vert_share = 0.5


def extended(block, sides, width):
    for axis, dim in sides:
        count = lax.axis_size(axis)
        forward = [(i, i + 1) for i in range(count - 1)]
        backward = [(target, source) for source, target in forward]
        low = lax.ppermute(
            lax.slice_in_dim(block, block.shape[dim] - width, None, axis=dim), axis, forward
        )
        high = lax.ppermute(lax.slice_in_dim(block, 0, width, axis=dim), axis, backward)
        block = jnp.concatenate([low, block, high], axis=dim)
    return block


def lookup(soil_class, soil_k):
    total = jnp.zeros(soil_class.shape, jnp.float32)
    for index in range(soil_k.shape[0]):
        total = total + jnp.where(soil_class == index, soil_k[index], 0.0)
    return total


def cholesky_lower(matrix):
    order = matrix.shape[0]
    places = jnp.arange(order, dtype=jnp.int32)

    def column_step(column, lower):
        onehot = (places == column.astype(jnp.int32)).astype(matrix.dtype)
        row_now = jnp.dot(onehot, lower, precision=lax.Precision.HIGHEST)
        remain = jnp.dot(matrix, onehot, precision=lax.Precision.HIGHEST) - jnp.dot(
            lower, row_now, precision=lax.Precision.HIGHEST
        )
        pivot = jnp.sqrt(jnp.sum(remain * onehot))
        fresh = jnp.where(
            places >= column.astype(jnp.int32), remain / pivot, jnp.zeros_like(remain)
        )
        return lower + fresh[:, None] * onehot[None, :]

    return lax.fori_loop(0, order, column_step, jnp.zeros_like(matrix))


def lower_inverse(lower):
    order = lower.shape[0]
    places = jnp.arange(order, dtype=jnp.int32)

    def row_step(row, solved):
        onehot = (places == row.astype(jnp.int32)).astype(lower.dtype)
        row_now = jnp.dot(onehot, lower, precision=lax.Precision.HIGHEST)
        pivot = jnp.sum(row_now * onehot)
        fresh = (onehot - jnp.dot(row_now, solved, precision=lax.Precision.HIGHEST)) / pivot
        return solved + onehot[:, None] * fresh[None, :]

    return lax.fori_loop(0, order, row_step, jnp.zeros_like(lower))


def update(padded, bordered_permeability, push):
    cond = bordered_permeability[None] * (0.5 + jax.nn.sigmoid(padded))
    center = padded[:, :, 1:-1, 1:-1]
    kcen = cond[:, :, 1:-1, 1:-1]
    flux = jnp.zeros_like(center)
    for rows, cols in (
        (slice(2, None), slice(1, -1)),
        (slice(None, -2), slice(1, -1)),
        (slice(1, -1), slice(2, None)),
        (slice(1, -1), slice(None, -2)),
    ):
        flux = flux + 0.5 * (kcen + cond[:, :, rows, cols]) * (padded[:, :, rows, cols] - center)
    upward = vert_share * 0.5 * (kcen[:, 1:] + kcen[:, :-1]) * (center[:, 1:] - center[:, :-1])
    flux = (
        flux
        + jnp.pad(upward, ((0, 0), (0, 1), (0, 0), (0, 0)))
        - jnp.pad(upward, ((0, 0), (1, 0), (0, 0), (0, 0)))
    )
    flux = flux + jnp.pad(push[:, None], ((0, 0), (0, center.shape[1] - 1), (0, 0), (0, 0)))
    return center + step_dt * flux


def propagate_pressure(state, bordered_permeability, infiltration_source):
    padded = extended(state, (("region", 2), ("tile", 3)), 1)
    return update(padded, bordered_permeability, infiltration_source)


def shards(
    prior_pressure,
    infiltration_source,
    soil_class,
    soil_k,
    obs_index,
    obs_value,
    obs_var,
    obs_count,
):
    realization_vectors = prior_pressure.shape[0]
    depth = 1
    bordered_permeability = extended(
        lookup(soil_class, soil_k), (("region", 1), ("tile", 2)), depth
    )
    predicted_pressure = prior_pressure
    for step in range(STEPS):
        predicted_pressure = propagate_pressure(
            predicted_pressure, bordered_permeability, infiltration_source
        )
    unrolled_vector = predicted_pressure.reshape(realization_vectors, -1)
    measured_pressure = jnp.take(unrolled_vector, obs_index, axis=1)
    live = (jnp.arange(obs_index.shape[0], dtype=jnp.int32) < obs_count[0]).astype(jnp.float32)
    weight = live / jnp.sqrt(obs_var)
    hmean = jnp.mean(measured_pressure, axis=0)
    anomal = (measured_pressure - hmean) * weight
    innov = (obs_value - hmean) * weight
    gram = jnp.dot(anomal, anomal.T, precision=lax.Precision.HIGHEST)
    bvec = jnp.dot(anomal, innov, precision=lax.Precision.HIGHEST)
    eye = jnp.eye(realization_vectors, dtype=jnp.float32)
    gram, bvec = lax.psum((gram, bvec), ("region", "tile"))
    lower = cholesky_lower((realization_vectors - 1.0) * eye + gram)
    inverse = lower_inverse(lower)
    wmean = jnp.dot(
        inverse.T,
        jnp.dot(inverse, bvec, precision=lax.Precision.HIGHEST),
        precision=lax.Precision.HIGHEST,
    )
    wroot = inverse.T * jnp.sqrt(realization_vectors - 1.0)
    blending_factor = wroot + wmean[:, None]
    sample_average = jnp.mean(predicted_pressure, axis=0)
    deviation_matrix = (predicted_pressure - sample_average).reshape(realization_vectors, -1)
    propagated_vector = jnp.dot(
        blending_factor.T, deviation_matrix, precision=lax.Precision.HIGHEST
    ).reshape(predicted_pressure.shape)
    return sample_average + propagated_vector


def solution(mesh):
    return jax.shard_map(
        shards,
        mesh=mesh,
        in_specs=(
            P(None, None, "region", "tile"),
            P(None, "region", "tile"),
            P(None, "region", "tile"),
            P(),
            P(("region", "tile")),
            P(("region", "tile")),
            P(("region", "tile")),
            P(("region", "tile")),
        ),
        out_specs=P(None, None, "region", "tile"),
        check_vma=False,
    )
```

profile of v0, /device:TPU:1, one launch (start us, length us, event | category | flops | bytes accessed | tf_op | source)
XLA Modules:
  0.0 435.6 jit_solution(1766568834195470314)
XLA Ops:
  0.0 1.8 fusion.141
  1.8 8.3 %select_add_fusion.1 = f32[4,4,128]{2,1,0:T(4,128)S(1)} fusion(s32[4,4,128]{2,1,0:T(4,128)} %param.14, f32[]{:T(128)} %bitcast.11, f32[]{:T(128)} %bitcast.10, f32[]{:T(128)} %bitcast.9, f32[]{:T(128)} %bitcast.8, f32[]{:T(128)} %bitcast.7, f32[]{:T(128)} %bitcast.6, f32[]{:T(128)} %bitcast.5, f32[]{:T(128)} %bitcast.4, f32[]{:T(128)} %bitcast.3, ...), kind=kLoop, calls=%fused_computation.194 | loop fusion | flops 71680 | bytes 16432 | tf_op jit(solution)/shard_map/add | solution.py:27
  10.1 4.6 %collective-permute-start = (f32[4,1,128]{2,1,0:T(1,128)S(1)}, f32[4,1,128]{2,1,0:T(1,128)S(1)}, u32[]{:S(2)}, u32[]{:S(2)}) collective-permute-start(f32[4,1,128]{2,1,0:T(1,128)S(1)} %get-tuple-element.244), channel_id=1, source_target_pairs={{0,32},{32,64},{64,96},{96,128},{128,160},{160,192},{192,224},{224... | collective-permute-start | bytes 6152 | tf_op jit(solution)/shard_map/ppermute | solution.py:16
  14.7 5.5 %collective-permute-start.1 = (f32[4,1,128]{2,1,0:T(1,128)S(1)}, f32[4,1,128]{2,1,0:T(1,128)S(1)}, u32[]{:S(2)}, u32[]{:S(2)}) collective-permute-start(f32[4,1,128]{2,1,0:T(1,128)S(1)} %get-tuple-element.245), channel_id=1, source_target_pairs={{32,0},{64,32},{96,64},{128,96},{160,128},{192,160},{224,192},{256... | collective-permute-start | bytes 6152 | tf_op jit(solution)/shard_map/ppermute | solution.py:19
  20.2 1.2 copy.59
  21.4 1.9 collective-permute-start.4
  23.3 2.4 collective-permute-start.5
  26.5 2.3 collective-permute-start.2
  28.8 1.3 collective-permute-start.3
  32.0 4.1 collective-permute-start.6
  36.3 1.3 collective-permute-start.7
  38.8 2.6 collective-permute-done.7
  43.5 1.0 fusion.48
  44.5 5.1 %collective-permute-start.8 = (f32[64,4,1,128]{3,0,2,1:T(8,128)S(1)}, f32[64,4,1,128]{3,0,2,1:T(8,128)S(1)}, u32[]{:S(2)}, u32[]{:S(2)}) collective-permute-start(f32[64,4,1,128]{3,0,2,1:T(8,128)S(1)} %get-tuple-element.238), channel_id=1, source_target_pairs={{0,32},{32,64},{64,96},{96,128},{128,160},{160,192},{192,224},{224... | collective-permute-start | bytes 393224 | tf_op jit(solution)/shard_map/ppermute | solution.py:16
  49.6 1.9 collective-permute-start.9
  51.5 4.3 collective-permute-done.9
  56.6 5.2 %collective-permute-start.10 = (f32[64,4,6,1]{0,1,3,2:T(4,128)S(1)}, f32[64,4,6,1]{0,1,3,2:T(4,128)S(1)}, u32[]{:S(2)}, u32[]{:S(2)}) collective-permute-start(f32[64,4,6,1]{0,1,3,2:T(4,128)S(1)} %copy.60), channel_id=1, source_target_pairs={{0,1},{1,2},{2,3},{3,4},{4,5},{5,6},{6,7},{7,8},{8,9},{9,10},{10,1... | collective-permute-start | bytes 18440 | tf_op jit(solution)/shard_map/ppermute | solution.py:16
  62.1 1.3 collective-permute-start.11
  63.7 4.3 collective-permute-done.11
  69.4 1.0 fusion.50
  70.4 2.9 collective-permute-start.12
  73.4 1.9 collective-permute-start.13
  75.3 4.3 collective-permute-done.13
  80.3 4.9 %collective-permute-start.14 = (f32[64,4,6,1]{0,1,3,2:T(4,128)S(1)}, f32[64,4,6,1]{0,1,3,2:T(4,128)S(1)}, u32[]{:S(2)}, u32[]{:S(2)}) collective-permute-start(f32[64,4,6,1]{0,1,3,2:T(4,128)S(1)} %copy.66), channel_id=1, source_target_pairs={{0,1},{1,2},{2,3},{3,4},{4,5},{5,6},{6,7},{7,8},{8,9},{9,10},{10,1... | collective-permute-start | bytes 18440 | tf_op jit(solution)/shard_map/ppermute | solution.py:16
  85.5 1.3 collective-permute-start.15
  87.8 2.4 collective-permute-done.15
  91.5 1.1 fusion.131
  94.9 106.0 %all-reduce.7 = (f32[64,64]{1,0:T(8,128)S(1)}, f32[64]{0:T(128)S(1)}) all-reduce(f32[64,64]{1,0:T(8,128)S(1)} %fusion.112, f32[64]{0:T(128)S(1)} %convolution_bitcast_fusion.6), channel_id=1, replica_groups=mesh['region'=16,'tile'=32] {'region','tile'}, use_global_device_ids=true, to_apply=%region_2.3 | all-reduce | flops 4160 | bytes 33280 | tf_op jit(solution)/shard_map/psum | solution.py:121
  200.9 120.4 %while.30 = (s32[]{:T(128)}, f32[64,64]{1,0:T(8,128)S(1)}, f32[64,64]{1,0:T(8,128)S(1)}, s32[]{:T(128)}, s32[]{:T(128)}) while((s32[]{:T(128)}, f32[64,64]{1,0:T(8,128)S(1)}, f32[64,64]{1,0:T(8,128)S(1)}, s32[]{:T(128)}, s32[]{:T(128)}) %tuple.90), condition=%wide.region_5.6_spmd.clone.clone, body=%wide.region_3.5_spmd.clone.clone.sunk | while | flops 168642 | bytes 84589 | solution.py:47
  203.0 0.8 fusion.173
  204.9 0.8 fusion.173
  208.6 0.8 fusion.173
  210.5 0.8 fusion.173
  214.3 0.8 fusion.173
  216.2 0.8 fusion.173
  219.9 0.8 fusion.173
  221.8 0.8 fusion.173
  223.7 0.8 fusion.173
  225.6 0.8 fusion.173
  227.4 0.8 fusion.173
  229.3 0.8 fusion.173
  233.1 0.8 fusion.173
  235.0 0.8 fusion.173
  238.7 0.8 fusion.173
  240.6 0.8 fusion.173
  244.4 0.8 fusion.173
  321.2 111.2 %while.29 = (s32[]{:T(128)}, f32[64,64]{1,0:T(8,128)S(1)}, f32[64,64]{1,0:T(8,128)S(1)}, s32[]{:T(128)}, s32[]{:T(128)}) while((s32[]{:T(128)}, f32[64,64]{1,0:T(8,128)S(1)}, f32[64,64]{1,0:T(8,128)S(1)}, s32[]{:T(128)}, s32[]{:T(128)}) %tuple.93), condition=%wide.region_8.9_spmd.clone, body=%wide.region_6.8_spmd.clone.sunk | while | flops 115330 | bytes 67164 | solution.py:61
  434.5 1.1 copy.76
  (710 shorter events, 187.8 us)
Async XLA Ops:
  0.0 30.1 %copy-start = (f32[64,4,4,128]{3,2,1,0:T(4,128)S(1)}, f32[64,4,4,128]{3,2,1,0:T(4,128)}, u32[]{:S(2)}) copy-start(f32[64,4,4,128]{3,2,1,0:T(4,128)} %param.12) | copy-start | bytes 1572868
  0.0 25.8 %copy-start.7 = (f32[64,4,128]{2,1,0:T(4,128)S(1)}, f32[64,4,128]{2,1,0:T(4,128)}, u32[]{:S(2)}) copy-start(f32[64,4,128]{2,1,0:T(4,128)} %param.13) | copy-start | bytes 393220
  10.1 15.7 %collective-permute-start = (f32[4,1,128]{2,1,0:T(1,128)S(1)}, f32[4,1,128]{2,1,0:T(1,128)S(1)}, u32[]{:S(2)}, u32[]{:S(2)}) collective-permute-start(f32[4,1,128]{2,1,0:T(1,128)S(1)} %get-tuple-element.244), channel_id=1, source_target_pairs={{0,32},{32,64},{64,96},{96,128},{128,160},{160,192},{192,224},{224... | collective-permute-start | bytes 6152 | tf_op jit(solution)/shard_map/ppermute | solution.py:16
  14.7 11.1 %collective-permute-start.1 = (f32[4,1,128]{2,1,0:T(1,128)S(1)}, f32[4,1,128]{2,1,0:T(1,128)S(1)}, u32[]{:S(2)}, u32[]{:S(2)}) collective-permute-start(f32[4,1,128]{2,1,0:T(1,128)S(1)} %get-tuple-element.245), channel_id=1, source_target_pairs={{32,0},{64,32},{96,64},{128,96},{160,128},{192,160},{224,192},{256... | collective-permute-start | bytes 6152 | tf_op jit(solution)/shard_map/ppermute | solution.py:19
  21.4 8.6 %collective-permute-start.4 = (f32[64,4,1,128]{3,0,2,1:T(8,128)S(1)}, f32[64,4,1,128]{3,0,2,1:T(8,128)S(1)}, u32[]{:S(2)}, u32[]{:S(2)}) collective-permute-start(f32[64,4,1,128]{3,0,2,1:T(8,128)S(1)} %get-tuple-element.241), channel_id=1, source_target_pairs={{0,32},{32,64},{64,96},{96,128},{128,160},{160,192},{192,224},{224... | collective-permute-start | bytes 393224 | tf_op jit(solution)/shard_map/ppermute | solution.py:16
  23.3 6.9 %collective-permute-start.5 = (f32[64,4,1,128]{3,0,2,1:T(8,128)S(1)}, f32[64,4,1,128]{3,0,2,1:T(8,128)S(1)}, u32[]{:S(2)}, u32[]{:S(2)}) collective-permute-start(f32[64,4,1,128]{3,0,2,1:T(8,128)S(1)} %get-tuple-element.240), channel_id=1, source_target_pairs={{32,0},{64,32},{96,64},{128,96},{160,128},{192,160},{224,192},{256... | collective-permute-start | bytes 393224 | tf_op jit(solution)/shard_map/ppermute | solution.py:19
  26.5 11.1 %collective-permute-start.2 = (f32[4,6,1]{2,1,0:T(8,128)}, f32[4,6,1]{2,1,0:T(8,128)}, u32[]{:S(2)}, u32[]{:S(2)}) collective-permute-start(f32[4,6,1]{2,1,0:T(8,128)} %get-tuple-element.242), channel_id=1, source_target_pairs={{0,1},{1,2},{2,3},{3,4},{4,5},{5,6},{6,7},{7,8},{8,9},{9,10},{10,1... | collective-permute-start | bytes 296 | tf_op jit(solution)/shard_map/ppermute | solution.py:16
  28.8 8.9 %collective-permute-start.3 = (f32[4,6,1]{2,1,0:T(8,128)}, f32[4,6,1]{2,1,0:T(8,128)}, u32[]{:S(2)}, u32[]{:S(2)}) collective-permute-start(f32[4,6,1]{2,1,0:T(8,128)} %get-tuple-element.243), channel_id=1, source_target_pairs={{1,0},{2,1},{3,2},{4,3},{5,4},{6,5},{7,6},{8,7},{9,8},{10,9},{11,1... | collective-permute-start | bytes 296 | tf_op jit(solution)/shard_map/ppermute | solution.py:19
  30.1 0.7 copy-start.3
  30.7 0.7 copy-start.5
  32.0 6.5 %collective-permute-start.6 = (f32[64,4,6,1]{0,1,3,2:T(4,128)S(1)}, f32[64,4,6,1]{0,1,3,2:T(4,128)S(1)}, u32[]{:S(2)}, u32[]{:S(2)}) collective-permute-start(f32[64,4,6,1]{0,1,3,2:T(4,128)S(1)} %copy.44), channel_id=1, source_target_pairs={{0,1},{1,2},{2,3},{3,4},{4,5},{5,6},{6,7},{7,8},{8,9},{9,10},{10,1... | collective-permute-start | bytes 18440 | tf_op jit(solution)/shard_map/ppermute | solution.py:16
  36.3 5.1 %collective-permute-start.7 = (f32[64,4,6,1]{0,1,3,2:T(4,128)S(1)}, f32[64,4,6,1]{0,1,3,2:T(4,128)S(1)}, u32[]{:S(2)}, u32[]{:S(2)}) collective-permute-start(f32[64,4,6,1]{0,1,3,2:T(4,128)S(1)} %copy.45), channel_id=1, source_target_pairs={{1,0},{2,1},{3,2},{4,3},{5,4},{6,5},{7,6},{8,7},{9,8},{10,9},{11,1... | collective-permute-start | bytes 18440 | tf_op jit(solution)/shard_map/ppermute | solution.py:19
  38.5 4.0 copy-start.1
  42.5 0.9 copy-start.4
  42.5 1.0 copy-start.6
  44.5 7.0 %collective-permute-start.8 = (f32[64,4,1,128]{3,0,2,1:T(8,128)S(1)}, f32[64,4,1,128]{3,0,2,1:T(8,128)S(1)}, u32[]{:S(2)}, u32[]{:S(2)}) collective-permute-start(f32[64,4,1,128]{3,0,2,1:T(8,128)S(1)} %get-tuple-element.238), channel_id=1, source_target_pairs={{0,32},{32,64},{64,96},{96,128},{128,160},{160,192},{192,224},{224... | collective-permute-start | bytes 393224 | tf_op jit(solution)/shard_map/ppermute | solution.py:16
  49.6 6.3 %collective-permute-start.9 = (f32[64,4,1,128]{3,0,2,1:T(8,128)S(1)}, f32[64,4,1,128]{3,0,2,1:T(8,128)S(1)}, u32[]{:S(2)}, u32[]{:S(2)}) collective-permute-start(f32[64,4,1,128]{3,0,2,1:T(8,128)S(1)} %get-tuple-element.239), channel_id=1, source_target_pairs={{32,0},{64,32},{96,64},{128,96},{160,128},{192,160},{224,192},{256... | collective-permute-start | bytes 393224 | tf_op jit(solution)/shard_map/ppermute | solution.py:19
  56.3 7.1 %copy-start.8 = (s32[256]{0:T(256)S(1)}, s32[256]{0:T(256)}, u32[]{:S(2)}) copy-start(s32[256]{0:T(256)} %param.16) | copy-start | bytes 3076
  56.3 12.1 %copy-start.2 = (f32[4,6,130]{2,1,0:T(8,128)S(1)}, f32[4,6,130]{2,1,0:T(8,128)}, u32[]{:S(2)}) copy-start(f32[4,6,130]{2,1,0:T(8,128)} %copy-done.1) | copy-start | bytes 37444
  56.6 6.8 %collective-permute-start.10 = (f32[64,4,6,1]{0,1,3,2:T(4,128)S(1)}, f32[64,4,6,1]{0,1,3,2:T(4,128)S(1)}, u32[]{:S(2)}, u32[]{:S(2)}) collective-permute-start(f32[64,4,6,1]{0,1,3,2:T(4,128)S(1)} %copy.60), channel_id=1, source_target_pairs={{0,1},{1,2},{2,3},{3,4},{4,5},{5,6},{6,7},{7,8},{8,9},{9,10},{10,1... | collective-permute-start | bytes 18440 | tf_op jit(solution)/shard_map/ppermute | solution.py:16
  62.1 5.9 %collective-permute-start.11 = (f32[64,4,6,1]{0,1,3,2:T(4,128)S(1)}, f32[64,4,6,1]{0,1,3,2:T(4,128)S(1)}, u32[]{:S(2)}, u32[]{:S(2)}) collective-permute-start(f32[64,4,6,1]{0,1,3,2:T(4,128)S(1)} %copy.61), channel_id=1, source_target_pairs={{1,0},{2,1},{3,2},{4,3},{5,4},{6,5},{7,6},{8,7},{9,8},{10,9},{11,1... | collective-permute-start | bytes 18440 | tf_op jit(solution)/shard_map/ppermute | solution.py:19
  70.4 4.9 %collective-permute-start.12 = (f32[64,4,1,128]{3,0,2,1:T(8,128)S(1)}, f32[64,4,1,128]{3,0,2,1:T(8,128)S(1)}, u32[]{:S(2)}, u32[]{:S(2)}) collective-permute-start(f32[64,4,1,128]{3,0,2,1:T(8,128)S(1)} %get-tuple-element.236), channel_id=1, source_target_pairs={{0,32},{32,64},{64,96},{96,128},{128,160},{160,192},{192,224},{224... | collective-permute-start | bytes 393224 | tf_op jit(solution)/shard_map/ppermute | solution.py:16
  73.4 6.3 %collective-permute-start.13 = (f32[64,4,1,128]{3,0,2,1:T(8,128)S(1)}, f32[64,4,1,128]{3,0,2,1:T(8,128)S(1)}, u32[]{:S(2)}, u32[]{:S(2)}) collective-permute-start(f32[64,4,1,128]{3,0,2,1:T(8,128)S(1)} %get-tuple-element.237), channel_id=1, source_target_pairs={{32,0},{64,32},{96,64},{128,96},{160,128},{192,160},{224,192},{256... | collective-permute-start | bytes 393224 | tf_op jit(solution)/shard_map/ppermute | solution.py:19
  80.3 7.1 %collective-permute-start.14 = (f32[64,4,6,1]{0,1,3,2:T(4,128)S(1)}, f32[64,4,6,1]{0,1,3,2:T(4,128)S(1)}, u32[]{:S(2)}, u32[]{:S(2)}) collective-permute-start(f32[64,4,6,1]{0,1,3,2:T(4,128)S(1)} %copy.66), channel_id=1, source_target_pairs={{0,1},{1,2},{2,3},{3,4},{4,5},{5,6},{6,7},{7,8},{8,9},{9,10},{10,1... | collective-permute-start | bytes 18440 | tf_op jit(solution)/shard_map/ppermute | solution.py:16
  85.5 4.7 %collective-permute-start.15 = (f32[64,4,6,1]{0,1,3,2:T(4,128)S(1)}, f32[64,4,6,1]{0,1,3,2:T(4,128)S(1)}, u32[]{:S(2)}, u32[]{:S(2)}) collective-permute-start(f32[64,4,6,1]{0,1,3,2:T(4,128)S(1)} %copy.67), channel_id=1, source_target_pairs={{1,0},{2,1},{3,2},{4,3},{5,4},{6,5},{7,6},{8,7},{9,8},{10,9},{11,1... | collective-permute-start | bytes 18440 | tf_op jit(solution)/shard_map/ppermute | solution.py:19
  92.6 1.3 copy-start.9
  92.6 1.3 copy-start.10
where the time goes:
time: 441 us; the launch traced here: 436 us
  matrix products  178 us (40%)
  blocking collectives  106 us (24%)
  starting transfers between devices  47.8 us (11%)
  loops' own time  45.1 us (10%)
  other arithmetic  26.4 us (6%)
  waiting for transfers between devices  18 us (4%)
  local copies, waits for them, and re-layouts  13.4 us (3%)
    psum x1, blocking collectives, shards(): gram, bvec = lax.psum((gram, bvec), ('region', 'tile'))  106 us
    dot_general x64, matrix products, column_step(): jnp.dot(lower, row_now, precision=lax.Precision.HIGHEST)  53.6 us
    dot_general x64, matrix products, row_step(): row_now = jnp.dot(onehot, lower, precision=lax.Precision.HIGHEST)  52.8 us
    dot_general x64, matrix products, row_step(): jnp.dot(row_now, solved, precision=lax.Precision.HIGHEST)  52.7 us
    another operation x1, loops' own time, cholesky_lower(): return lax.fori_loop(0, order, column_step, jnp.zeros_like(matrix))  44.6 us
    ppermute x8, starting transfers between devices, extended(): lax.ppermute(lax.slice_in_dim(block, block.shape[dim] - width, None, axis...  30.9 us
    ppermute x8, waiting for transfers between devices, extended(): lax.ppermute(lax.slice_in_dim(block, 0, width, axis=dim), axis, backward)  17.9 us
    ppermute x8, starting transfers between devices, extended(): lax.ppermute(lax.slice_in_dim(block, 0, width, axis=dim), axis, backward)  16.9 us
  transfers between devices with their start and end apart: 16, of which 5 were waited for; matrix products, arithmetic and copies ran while one was open for 1% of the time, Pallas kernels for 0%

commit v1 on v0

--- a/solution.py
+++ b/solution.py
@@ -118,7 +118,7 @@
     gram = jnp.dot(anomal, anomal.T, precision=lax.Precision.HIGHEST)
     bvec = jnp.dot(anomal, innov, precision=lax.Precision.HIGHEST)
     eye = jnp.eye(realization_vectors, dtype=jnp.float32)
-    gram, bvec = lax.psum((gram, bvec), ("region", "tile"))
+    gram, bvec = lax.psum(lax.psum((gram, bvec), axis_name="region"), axis_name="tile")
     lower = cholesky_lower((realization_vectors - 1.0) * eye + gram)
     inverse = lower_inverse(lower)
     wmean = jnp.dot(

time: 441 us -> 515 us (1.17)
  the two profiles are of different devices: /device:TPU:1 before, /device:TPU:32 now
where the time goes in v1:
time: 515 us; the launch traced here: 513 us
  blocking collectives  187 us (36%)
  matrix products  168 us (33%)
  starting transfers between devices  52.3 us (10%)
  loops' own time  47.6 us (9%)
  other arithmetic  26.4 us (5%)
  waiting for transfers between devices  16.7 us (3%)
  local copies, waits for them, and re-layouts  13.4 us (3%)
    psum x1, blocking collectives, shards(): lax.psum(lax.psum((gram, bvec), axis_name='region'), axis_name='tile')  139 us
    dot_general x64, matrix products, column_step(): jnp.dot(lower, row_now, precision=lax.Precision.HIGHEST)  56.3 us
    dot_general x64, matrix products, row_step(): row_now = jnp.dot(onehot, lower, precision=lax.Precision.HIGHEST)  47.9 us
    psum x1, blocking collectives, shards(): lax.psum((gram, bvec), axis_name='region')  47.6 us
    another operation x1, loops' own time, cholesky_lower(): return lax.fori_loop(0, order, column_step, jnp.zeros_like(matrix))  47.2 us
    dot_general x64, matrix products, row_step(): jnp.dot(row_now, solved, precision=lax.Precision.HIGHEST)  45.2 us
    ppermute x8, starting transfers between devices, extended(): lax.ppermute(lax.slice_in_dim(block, block.shape[dim] - width, None, axis...  27.7 us
    ppermute x8, starting transfers between devices, extended(): lax.ppermute(lax.slice_in_dim(block, 0, width, axis=dim), axis, backward)  24.6 us
  transfers between devices with their start and end apart: 16, of which 7 were waited for; matrix products, arithmetic and copies ran while one was open for 1% of the time, Pallas kernels for 0%

profile of v1, /device:TPU:32, one launch (start us, length us, event | category | flops | bytes accessed | tf_op | source)
XLA Modules:
  0.0 512.6 jit_solution(3313087581010857931)
XLA Ops:
  0.0 1.8 fusion.141
  1.8 8.3 %select_add_fusion.1 = f32[4,4,128]{2,1,0:T(4,128)S(1)} fusion(s32[4,4,128]{2,1,0:T(4,128)} %param.14, f32[]{:T(128)} %bitcast.11, f32[]{:T(128)} %bitcast.10, f32[]{:T(128)} %bitcast.9, f32[]{:T(128)} %bitcast.8, f32[]{:T(128)} %bitcast.7, f32[]{:T(128)} %bitcast.6, f32[]{:T(128)} %bitcast.5, f32[]{:T(128)} %bitcast.4, f32[]{:T(128)} %bitcast.3, ...), kind=kLoop, calls=%fused_computation.194 | loop fusion | flops 71680 | bytes 16432 | tf_op jit(solution)/shard_map/add | solution.py:27
  10.1 1.9 collective-permute-start
  12.0 4.9 collective-permute-start.1
  16.9 1.2 copy.59
  18.1 1.9 collective-permute-start.4
  20.0 4.9 collective-permute-start.5
  25.6 4.9 collective-permute-start.2
  30.5 1.3 collective-permute-start.3
  33.7 4.6 collective-permute-start.6
  38.6 1.3 collective-permute-start.7
  41.1 3.2 collective-permute-done.7
  46.3 1.0 fusion.48
  47.4 1.9 collective-permute-start.8
  49.3 4.9 collective-permute-start.9
  54.9 1.8 collective-permute-done.9
  57.4 5.5 %collective-permute-start.10 = (f32[64,4,6,1]{0,1,3,2:T(4,128)S(1)}, f32[64,4,6,1]{0,1,3,2:T(4,128)S(1)}, u32[]{:S(2)}, u32[]{:S(2)}) collective-permute-start(f32[64,4,6,1]{0,1,3,2:T(4,128)S(1)} %copy.60), channel_id=1, source_target_pairs={{0,1},{1,2},{2,3},{3,4},{4,5},{5,6},{6,7},{7,8},{8,9},{9,10},{10,1... | collective-permute-start | bytes 18440 | tf_op jit(solution)/shard_map/ppermute | solution.py:16
  63.2 1.3 collective-permute-start.11
  64.8 5.1 %collective-permute-done.11 = f32[64,4,6,1]{0,1,3,2:T(4,128)S(1)} collective-permute-done((f32[64,4,6,1]{0,1,3,2:T(4,128)S(1)}, f32[64,4,6,1]{0,1,3,2:T(4,128)S(1)}, u32[]{:S(2)}, u32[]{:S(2)}) %collective-permute-start.11) | collective-permute-done | bytes 6176 | tf_op jit(solution)/shard_map/ppermute | solution.py:19
  71.3 1.0 fusion.50
  72.4 1.9 collective-permute-start.12
  74.3 4.9 collective-permute-start.13
  79.9 1.8 collective-permute-done.13
  82.4 5.1 %collective-permute-start.14 = (f32[64,4,6,1]{0,1,3,2:T(4,128)S(1)}, f32[64,4,6,1]{0,1,3,2:T(4,128)S(1)}, u32[]{:S(2)}, u32[]{:S(2)}) collective-permute-start(f32[64,4,6,1]{0,1,3,2:T(4,128)S(1)} %copy.66), channel_id=1, source_target_pairs={{0,1},{1,2},{2,3},{3,4},{4,5},{5,6},{6,7},{7,8},{8,9},{9,10},{10,1... | collective-permute-start | bytes 18440 | tf_op jit(solution)/shard_map/ppermute | solution.py:16
  87.8 1.3 collective-permute-start.15
  90.1 3.3 collective-permute-done.15
  94.7 1.1 fusion.131
  98.0 47.6 %all-reduce.8 = (f32[64,64]{1,0:T(8,128)S(1)}, f32[64]{0:T(128)S(1)}) all-reduce(f32[64,64]{1,0:T(8,128)S(1)} %fusion.112, f32[64]{0:T(128)S(1)} %convolution_bitcast_fusion.6), channel_id=1, replica_groups=mesh['region'=16,'tile'=32] {'region'}, use_global_device_ids=true, to_apply=%region_2.3 | all-reduce | flops 4160 | bytes 33280 | tf_op jit(solution)/shard_map/psum | solution.py:121
  145.6 139.4 %all-reduce.7 = (f32[64,64]{1,0:T(8,128)S(1)}, f32[64]{0:T(128)S(1)}) all-reduce(f32[64,64]{1,0:T(8,128)S(1)} %get-tuple-element.222, f32[64]{0:T(128)S(1)} %get-tuple-element.223), channel_id=1, replica_groups=mesh['region'=16,'tile'=32] {'tile'}, use_global_device_ids=true, to_apply=%region_3.4 | all-reduce | flops 4160 | bytes 33280 | tf_op jit(solution)/shard_map/psum | solution.py:121
  285.0 125.6 %while.30 = (s32[]{:T(128)}, f32[64,64]{1,0:T(8,128)S(1)}, f32[64,64]{1,0:T(8,128)S(1)}, s32[]{:T(128)}, s32[]{:T(128)}) while((s32[]{:T(128)}, f32[64,64]{1,0:T(8,128)S(1)}, f32[64,64]{1,0:T(8,128)S(1)}, s32[]{:T(128)}, s32[]{:T(128)}) %tuple.90), condition=%wide.region_6.7_spmd.clone.clone, body=%wide.region_4.6_spmd.clone.clone.sunk | while | flops 168642 | bytes 84589 | solution.py:47
  289.2 0.9 fusion.173
  295.1 0.9 fusion.173
  297.1 0.9 fusion.173
  302.9 0.9 fusion.173
  304.9 0.9 fusion.173
  310.8 0.9 fusion.173
  318.6 0.9 fusion.173
  326.5 0.9 fusion.173
  332.4 0.9 fusion.173
  334.3 0.9 fusion.173
  340.2 0.9 fusion.173
  342.2 0.9 fusion.173
  348.1 0.9 fusion.173
  355.9 0.9 fusion.173
  363.8 0.9 fusion.173
  369.7 0.9 fusion.173
  410.6 98.8 %while.29 = (s32[]{:T(128)}, f32[64,64]{1,0:T(8,128)S(1)}, f32[64,64]{1,0:T(8,128)S(1)}, s32[]{:T(128)}, s32[]{:T(128)}) while((s32[]{:T(128)}, f32[64,64]{1,0:T(8,128)S(1)}, f32[64,64]{1,0:T(8,128)S(1)}, s32[]{:T(128)}, s32[]{:T(128)}) %tuple.93), condition=%wide.region_9.10_spmd.clone, body=%wide.region_7.9_spmd.clone.sunk | while | flops 115330 | bytes 67164 | solution.py:61
  511.4 1.1 copy.76
  (711 shorter events, 179.6 us)
Async XLA Ops:
  0.0 31.8 %copy-start = (f32[64,4,4,128]{3,2,1,0:T(4,128)S(1)}, f32[64,4,4,128]{3,2,1,0:T(4,128)}, u32[]{:S(2)}) copy-start(f32[64,4,4,128]{3,2,1,0:T(4,128)} %param.12) | copy-start | bytes 1572868
  0.0 24.9 %copy-start.7 = (f32[64,4,128]{2,1,0:T(4,128)S(1)}, f32[64,4,128]{2,1,0:T(4,128)}, u32[]{:S(2)}) copy-start(f32[64,4,128]{2,1,0:T(4,128)} %param.13) | copy-start | bytes 393220
  10.1 14.9 %collective-permute-start = (f32[4,1,128]{2,1,0:T(1,128)S(1)}, f32[4,1,128]{2,1,0:T(1,128)S(1)}, u32[]{:S(2)}, u32[]{:S(2)}) collective-permute-start(f32[4,1,128]{2,1,0:T(1,128)S(1)} %get-tuple-element.246), channel_id=1, source_target_pairs={{0,32},{32,64},{64,96},{96,128},{128,160},{160,192},{192,224},{224... | collective-permute-start | bytes 6152 | tf_op jit(solution)/shard_map/ppermute | solution.py:16
  12.0 12.9 %collective-permute-start.1 = (f32[4,1,128]{2,1,0:T(1,128)S(1)}, f32[4,1,128]{2,1,0:T(1,128)S(1)}, u32[]{:S(2)}, u32[]{:S(2)}) collective-permute-start(f32[4,1,128]{2,1,0:T(1,128)S(1)} %get-tuple-element.247), channel_id=1, source_target_pairs={{32,0},{64,32},{96,64},{128,96},{160,128},{192,160},{224,192},{256... | collective-permute-start | bytes 6152 | tf_op jit(solution)/shard_map/ppermute | solution.py:19
  18.1 13.7 %collective-permute-start.4 = (f32[64,4,1,128]{3,0,2,1:T(8,128)S(1)}, f32[64,4,1,128]{3,0,2,1:T(8,128)S(1)}, u32[]{:S(2)}, u32[]{:S(2)}) collective-permute-start(f32[64,4,1,128]{3,0,2,1:T(8,128)S(1)} %get-tuple-element.243), channel_id=1, source_target_pairs={{0,32},{32,64},{64,96},{96,128},{128,160},{160,192},{192,224},{224... | collective-permute-start | bytes 393224 | tf_op jit(solution)/shard_map/ppermute | solution.py:16
  20.0 12.0 %collective-permute-start.5 = (f32[64,4,1,128]{3,0,2,1:T(8,128)S(1)}, f32[64,4,1,128]{3,0,2,1:T(8,128)S(1)}, u32[]{:S(2)}, u32[]{:S(2)}) collective-permute-start(f32[64,4,1,128]{3,0,2,1:T(8,128)S(1)} %get-tuple-element.242), channel_id=1, source_target_pairs={{32,0},{64,32},{96,64},{128,96},{160,128},{192,160},{224,192},{256... | collective-permute-start | bytes 393224 | tf_op jit(solution)/shard_map/ppermute | solution.py:19
  25.6 14.2 %collective-permute-start.2 = (f32[4,6,1]{2,1,0:T(8,128)}, f32[4,6,1]{2,1,0:T(8,128)}, u32[]{:S(2)}, u32[]{:S(2)}) collective-permute-start(f32[4,6,1]{2,1,0:T(8,128)} %get-tuple-element.244), channel_id=1, source_target_pairs={{0,1},{1,2},{2,3},{3,4},{4,5},{5,6},{6,7},{7,8},{8,9},{9,10},{10,1... | collective-permute-start | bytes 296 | tf_op jit(solution)/shard_map/ppermute | solution.py:16
  30.5 9.4 %collective-permute-start.3 = (f32[4,6,1]{2,1,0:T(8,128)}, f32[4,6,1]{2,1,0:T(8,128)}, u32[]{:S(2)}, u32[]{:S(2)}) collective-permute-start(f32[4,6,1]{2,1,0:T(8,128)} %get-tuple-element.245), channel_id=1, source_target_pairs={{1,0},{2,1},{3,2},{4,3},{5,4},{6,5},{7,6},{8,7},{9,8},{10,9},{11,1... | collective-permute-start | bytes 296 | tf_op jit(solution)/shard_map/ppermute | solution.py:19
  31.8 0.7 copy-start.3
  32.5 0.7 copy-start.5
  33.7 7.0 %collective-permute-start.6 = (f32[64,4,6,1]{0,1,3,2:T(4,128)S(1)}, f32[64,4,6,1]{0,1,3,2:T(4,128)S(1)}, u32[]{:S(2)}, u32[]{:S(2)}) collective-permute-start(f32[64,4,6,1]{0,1,3,2:T(4,128)S(1)} %copy.44), channel_id=1, source_target_pairs={{0,1},{1,2},{2,3},{3,4},{4,5},{5,6},{6,7},{7,8},{8,9},{9,10},{10,1... | collective-permute-start | bytes 18440 | tf_op jit(solution)/shard_map/ppermute | solution.py:16
  38.6 5.7 %collective-permute-start.7 = (f32[64,4,6,1]{0,1,3,2:T(4,128)S(1)}, f32[64,4,6,1]{0,1,3,2:T(4,128)S(1)}, u32[]{:S(2)}, u32[]{:S(2)}) collective-permute-start(f32[64,4,6,1]{0,1,3,2:T(4,128)S(1)} %copy.45), channel_id=1, source_target_pairs={{1,0},{2,1},{3,2},{4,3},{5,4},{6,5},{7,6},{8,7},{9,8},{10,9},{11,1... | collective-permute-start | bytes 18440 | tf_op jit(solution)/shard_map/ppermute | solution.py:19
  40.7 4.6 copy-start.1
  45.4 0.9 copy-start.4
  45.4 1.0 copy-start.6
  47.4 7.5 %collective-permute-start.8 = (f32[64,4,1,128]{3,0,2,1:T(8,128)S(1)}, f32[64,4,1,128]{3,0,2,1:T(8,128)S(1)}, u32[]{:S(2)}, u32[]{:S(2)}) collective-permute-start(f32[64,4,1,128]{3,0,2,1:T(8,128)S(1)} %get-tuple-element.240), channel_id=1, source_target_pairs={{0,32},{32,64},{64,96},{96,128},{128,160},{160,192},{192,224},{224... | collective-permute-start | bytes 393224 | tf_op jit(solution)/shard_map/ppermute | solution.py:16
  49.3 7.4 %collective-permute-start.9 = (f32[64,4,1,128]{3,0,2,1:T(8,128)S(1)}, f32[64,4,1,128]{3,0,2,1:T(8,128)S(1)}, u32[]{:S(2)}, u32[]{:S(2)}) collective-permute-start(f32[64,4,1,128]{3,0,2,1:T(8,128)S(1)} %get-tuple-element.241), channel_id=1, source_target_pairs={{32,0},{64,32},{96,64},{128,96},{160,128},{192,160},{224,192},{256... | collective-permute-start | bytes 393224 | tf_op jit(solution)/shard_map/ppermute | solution.py:19
  57.1 7.4 %copy-start.8 = (s32[256]{0:T(256)S(1)}, s32[256]{0:T(256)}, u32[]{:S(2)}) copy-start(s32[256]{0:T(256)} %param.16) | copy-start | bytes 3076
  57.1 13.2 %copy-start.2 = (f32[4,6,130]{2,1,0:T(8,128)S(1)}, f32[4,6,130]{2,1,0:T(8,128)}, u32[]{:S(2)}) copy-start(f32[4,6,130]{2,1,0:T(8,128)} %copy-done.1) | copy-start | bytes 37444
  57.4 7.1 %collective-permute-start.10 = (f32[64,4,6,1]{0,1,3,2:T(4,128)S(1)}, f32[64,4,6,1]{0,1,3,2:T(4,128)S(1)}, u32[]{:S(2)}, u32[]{:S(2)}) collective-permute-start(f32[64,4,6,1]{0,1,3,2:T(4,128)S(1)} %copy.60), channel_id=1, source_target_pairs={{0,1},{1,2},{2,3},{3,4},{4,5},{5,6},{6,7},{7,8},{8,9},{9,10},{10,1... | collective-permute-start | bytes 18440 | tf_op jit(solution)/shard_map/ppermute | solution.py:16
  63.2 6.8 %collective-permute-start.11 = (f32[64,4,6,1]{0,1,3,2:T(4,128)S(1)}, f32[64,4,6,1]{0,1,3,2:T(4,128)S(1)}, u32[]{:S(2)}, u32[]{:S(2)}) collective-permute-start(f32[64,4,6,1]{0,1,3,2:T(4,128)S(1)} %copy.61), channel_id=1, source_target_pairs={{1,0},{2,1},{3,2},{4,3},{5,4},{6,5},{7,6},{8,7},{9,8},{10,9},{11,1... | collective-permute-start | bytes 18440 | tf_op jit(solution)/shard_map/ppermute | solution.py:19
  72.4 7.5 %collective-permute-start.12 = (f32[64,4,1,128]{3,0,2,1:T(8,128)S(1)}, f32[64,4,1,128]{3,0,2,1:T(8,128)S(1)}, u32[]{:S(2)}, u32[]{:S(2)}) collective-permute-start(f32[64,4,1,128]{3,0,2,1:T(8,128)S(1)} %get-tuple-element.238), channel_id=1, source_target_pairs={{0,32},{32,64},{64,96},{96,128},{128,160},{160,192},{192,224},{224... | collective-permute-start | bytes 393224 | tf_op jit(solution)/shard_map/ppermute | solution.py:16
  74.3 7.4 %collective-permute-start.13 = (f32[64,4,1,128]{3,0,2,1:T(8,128)S(1)}, f32[64,4,1,128]{3,0,2,1:T(8,128)S(1)}, u32[]{:S(2)}, u32[]{:S(2)}) collective-permute-start(f32[64,4,1,128]{3,0,2,1:T(8,128)S(1)} %get-tuple-element.239), channel_id=1, source_target_pairs={{32,0},{64,32},{96,64},{128,96},{160,128},{192,160},{224,192},{256... | collective-permute-start | bytes 393224 | tf_op jit(solution)/shard_map/ppermute | solution.py:19
  82.4 7.4 %collective-permute-start.14 = (f32[64,4,6,1]{0,1,3,2:T(4,128)S(1)}, f32[64,4,6,1]{0,1,3,2:T(4,128)S(1)}, u32[]{:S(2)}, u32[]{:S(2)}) collective-permute-start(f32[64,4,6,1]{0,1,3,2:T(4,128)S(1)} %copy.66), channel_id=1, source_target_pairs={{0,1},{1,2},{2,3},{3,4},{4,5},{5,6},{6,7},{7,8},{8,9},{9,10},{10,1... | collective-permute-start | bytes 18440 | tf_op jit(solution)/shard_map/ppermute | solution.py:16
  87.8 5.6 %collective-permute-start.15 = (f32[64,4,6,1]{0,1,3,2:T(4,128)S(1)}, f32[64,4,6,1]{0,1,3,2:T(4,128)S(1)}, u32[]{:S(2)}, u32[]{:S(2)}) collective-permute-start(f32[64,4,6,1]{0,1,3,2:T(4,128)S(1)} %copy.67), channel_id=1, source_target_pairs={{1,0},{2,1},{3,2},{4,3},{5,4},{6,5},{7,6},{8,7},{9,8},{10,9},{11,1... | collective-permute-start | bytes 18440 | tf_op jit(solution)/shard_map/ppermute | solution.py:19
  95.8 1.3 copy-start.9
  95.8 1.3 copy-start.10
